TPU v7x, 128 devices: a whole 4x4x4 slice. The times are simulated.
128 devices in a mesh: gx: 8 (over x, core), gy: 16 (over y, z).
Axes of the slice: x: 4, y: 4, z: 4, core: 2. Of those that a mesh axis runs over, the one named last changes fastest.
Arguments:
- pressure_source: float32 [192, 384, 384], P('gx', 'gy'), may hold values from -6 to 6
- building_heights: int32 [32, 64], replicated, may hold values from 0 to 63
Outputs:
- correction: float32 [192, 384, 384], P('gx', 'gy')
- coarse_solution: float32 [64, 128, 128], P('gx', 'gy')
Inputs may be any that keep to these rules, and one draw needn't show every extreme that they name: `building_heights`: the height of the building in each element column, in elements, so that the top layer of every column is fluid.
All inputs are finite; a program needn't handle non-finite values.
Results may differ from a plain program's by a relative error of at most 0.0003.
Values sent between devices are 32-bit elements; how exact they have to be, the bound alone decides.
No kernel may reach another device: no remote copies, remote signals or barrier semaphores. Data moves between devices by JAX's collectives and lax.ppermute only.
A program may use at most 128 MiB of HBM per device.

v0:
```python
import jax
import jax.numpy as jnp
import numpy as np
from jax import lax
from jax.sharding import PartitionSpec as P

CG_ITERS = 10
HIGHEST = lax.Precision.HIGHEST


def with_halo(cells, sides, width):
    for axis, dim in sides:
        count = lax.axis_size(axis)
        ends = count - 1
        head = lax.slice_in_dim(cells, 0, width, axis=dim)
        tail = lax.slice_in_dim(cells, cells.shape[dim] - width, cells.shape[dim], axis=dim)
        cells = jnp.concatenate(
            [
                lax.ppermute(tail, axis, [(i, (i + 1) % count) for i in range(ends)]),
                cells,
                lax.ppermute(head, axis, [((i + 1) % count, i) for i in range(ends)]),
            ],
            axis=dim,
        )
    return cells


def gll_nodes(node_count):
    if node_count == 6:
        outer_point = 0.7650553239294647
        inner_point = 0.2852315164806451
        points = [-1.0, -outer_point, -inner_point, inner_point, outer_point, 1.0]
        weights = [
            1.0 / 15.0,
            0.378474956297847,
            0.5548583770354863,
            0.5548583770354863,
            0.378474956297847,
            1.0 / 15.0,
        ]
    elif node_count == 4:
        inner_point = 0.4472135954999579
        points = [-1.0, -inner_point, inner_point, 1.0]
        weights = [1.0 / 6.0, 5.0 / 6.0, 5.0 / 6.0, 1.0 / 6.0]
    else:
        points = [-1.0, 1.0]
        weights = [1.0, 1.0]
    return (np.array(points), np.array(weights))


def diagonal_of(matrix):
    return np.array([matrix[index_id, index_id] for index_id in range(matrix.shape[0])])


def lagrange_tables(node_count):
    points, weights = gll_nodes(node_count)
    others = [
        [points[col_id] - points[other] for other in range(node_count) if other != col_id]
        for col_id in range(node_count)
    ]
    bary_weights = np.array([1.0 / np.prod(entries) for entries in others])
    derivative = np.zeros((node_count, node_count))
    for row_id in range(node_count):
        for col_id in range(node_count):
            if row_id != col_id:
                derivative[row_id, col_id] = (
                    bary_weights[col_id] / bary_weights[row_id] / (points[row_id] - points[col_id])
                )
        derivative[row_id, row_id] = -np.sum(derivative[row_id])
    stiffness = derivative.T @ (weights[:, None] * derivative)
    return (stiffness, weights)


def interpolation(coarse_count, fine_count):
    coarse_points = gll_nodes(coarse_count)[0]
    fine_points = gll_nodes(fine_count)[0]
    matrix = np.ones((fine_count, coarse_count))
    for row_id in range(fine_count):
        for col_id in range(coarse_count):
            for other in range(coarse_count):
                if other != col_id:
                    matrix[row_id, col_id] *= (fine_points[row_id] - coarse_points[other]) / (
                        coarse_points[col_id] - coarse_points[other]
                    )
    return matrix


def chebyshev_bounds(node_count):
    stiffness, weights = lagrange_tables(node_count)
    row_abs = np.abs(stiffness).sum(axis=1)
    diag_vals = diagonal_of(stiffness)
    wide_one = weights[:, None, None]
    wide_two = weights[None, :, None]
    wide_three = weights[None, None, :]
    numerator = (
        row_abs[:, None, None] * wide_two * wide_three
        + wide_one * row_abs[None, :, None] * wide_three
        + wide_one * wide_two * row_abs[None, None, :]
    )
    denominator = (
        diag_vals[:, None, None] * wide_two * wide_three
        + wide_one * diag_vals[None, :, None] * wide_three
        + wide_one * wide_two * diag_vals[None, None, :]
    )
    top_bound = float(np.max(numerator / denominator))
    return (top_bound, 0.1 * top_bound)


def tiled(vector, length, position):
    repeated = jnp.asarray(np.tile(vector, length // vector.shape[0]), jnp.float32)
    return repeated.reshape(tuple((length if axis_id == position else 1 for axis_id in range(3))))


def along_first(values, matrix):
    out_count, in_count = matrix.shape
    blocks = values.shape[0] // in_count
    shaped = values.reshape(blocks, in_count, values.shape[1] * values.shape[2])
    result = jnp.einsum("ip,xpr->xir", jnp.asarray(matrix, jnp.float32), shaped, precision=HIGHEST)
    return result.reshape(blocks * out_count, values.shape[1], values.shape[2])


def along_second(values, matrix):
    out_count, in_count = matrix.shape
    blocks = values.shape[1] // in_count
    shaped = values.reshape(values.shape[0], blocks, in_count, values.shape[2])
    result = jnp.einsum(
        "jq,xyqc->xyjc", jnp.asarray(matrix, jnp.float32), shaped, precision=HIGHEST
    )
    return result.reshape(values.shape[0], blocks * out_count, values.shape[2])


def along_third(values, matrix):
    out_count, in_count = matrix.shape
    blocks = values.shape[2] // in_count
    block_matrix = jnp.asarray(np.kron(np.eye(blocks), matrix.T), jnp.float32)
    result = jnp.dot(values.reshape(-1, values.shape[2]), block_matrix, precision=HIGHEST)
    return result.reshape(values.shape[0], values.shape[1], blocks * out_count)


def pass_first(padded, node_count):
    position = np.arange(padded.shape[0] - 2) % node_count
    at_start = jnp.asarray(position == 0, jnp.float32)[:, None, None]
    at_end = jnp.asarray(position == node_count - 1, jnp.float32)[:, None, None]
    return padded[1:-1] + at_start * padded[:-2] + at_end * padded[2:]


def pass_second(padded, node_count):
    position = np.arange(padded.shape[1] - 2) % node_count
    at_start = jnp.asarray(position == 0, jnp.float32)[None, :, None]
    at_end = jnp.asarray(position == node_count - 1, jnp.float32)[None, :, None]
    return padded[:, 1:-1] + at_start * padded[:, :-2] + at_end * padded[:, 2:]


def pass_third(values, node_count):
    position = np.arange(values.shape[2]) % node_count
    at_start = jnp.asarray(position == 0, jnp.float32)[None, None, :]
    at_end = jnp.asarray(position == node_count - 1, jnp.float32)[None, None, :]
    earlier = jnp.pad(values[:, :, :-1], ((0, 0), (0, 0), (1, 0)))
    following = jnp.pad(values[:, :, 1:], ((0, 0), (0, 0), (0, 1)))
    return values + at_start * earlier + at_end * following


def rim_joint(values):
    return with_halo(values, (("gx", 0), ("gy", 1)), 1)


def assemble(values, node_count):
    summed = pass_third(values, node_count)
    padded = rim_joint(summed)
    return pass_second(pass_first(padded, node_count), node_count)


def spread_counts(elem_pad, node_count):
    position = np.arange(node_count)
    at_start = jnp.asarray(position == 0, jnp.float32)
    at_end = jnp.asarray(position == node_count - 1, jnp.float32)
    step_one = (
        elem_pad[1:-1][:, None]
        + at_start[None, :, None, None] * elem_pad[:-2][:, None]
        + at_end[None, :, None, None] * elem_pad[2:][:, None]
    )
    step_one = step_one.reshape(-1, elem_pad.shape[1], elem_pad.shape[2])
    step_two = (
        step_one[:, 1:-1][:, :, None]
        + at_start[None, None, :, None] * step_one[:, :-2][:, :, None]
        + at_end[None, None, :, None] * step_one[:, 2:][:, :, None]
    )
    step_two = step_two.reshape(step_one.shape[0], -1, elem_pad.shape[2])
    step_three = (
        step_two[:, :, 1:-1][:, :, :, None]
        + at_start * step_two[:, :, :-2][:, :, :, None]
        + at_end * step_two[:, :, 2:][:, :, :, None]
    )
    return step_three.reshape(step_two.shape[0], step_two.shape[1], -1)


def level_data(fluid_pad, exist_pad, node_count):
    fluid_count = spread_counts(fluid_pad, node_count)
    exist_count = spread_counts(exist_pad, node_count)
    ground = jnp.asarray(np.arange(fluid_count.shape[2]) > 0, jnp.float32)[None, None, :]
    node_mask = (
        (fluid_count == exist_count).astype(jnp.float32)
        * (fluid_count > 0.5).astype(jnp.float32)
        * ground
    )
    node_weight = 1.0 / exist_count
    fluid_cells = fluid_pad[1:-1, 1:-1, 1:-1]
    fluid_node = jnp.repeat(
        jnp.repeat(jnp.repeat(fluid_cells, node_count, axis=0), node_count, axis=1),
        node_count,
        axis=2,
    )
    stiffness, weights = lagrange_tables(node_count)
    stiff_diag = diagonal_of(stiffness)
    dims_now = fluid_count.shape
    local_diag = (
        tiled(stiff_diag, dims_now[0], 0)
        * tiled(weights, dims_now[1], 1)
        * tiled(weights, dims_now[2], 2)
    )
    local_diag = local_diag + tiled(weights, dims_now[0], 0) * tiled(
        stiff_diag, dims_now[1], 1
    ) * tiled(weights, dims_now[2], 2)
    local_diag = local_diag + tiled(weights, dims_now[0], 0) * tiled(
        weights, dims_now[1], 1
    ) * tiled(stiff_diag, dims_now[2], 2)
    inverse_diag = node_mask / (fluid_count * local_diag + 1.0 - node_mask)
    return (node_count, fluid_node, node_mask, node_weight, inverse_diag)


def element_action(values, level_info):
    node_count, fluid_node = (level_info[0], level_info[1])
    stiffness, weights = lagrange_tables(node_count)
    mass_first = tiled(weights, values.shape[0], 0)
    mass_second = tiled(weights, values.shape[1], 1)
    mass_third = tiled(weights, values.shape[2], 2)
    summed_terms = mass_second * mass_third * along_first(values, stiffness)
    summed_terms = summed_terms + mass_first * mass_third * along_second(values, stiffness)
    summed_terms = summed_terms + mass_first * mass_second * along_third(values, stiffness)
    return fluid_node * summed_terms


def apply_operator(values, level_info, assembler):
    return level_info[2] * assembler(element_action(values, level_info), level_info[0])


def smooth(target, start, level_info, bounds, assembler, from_zero):
    top_bound, low_bound = bounds
    center = 0.5 * (top_bound + low_bound)
    half_width = 0.5 * (top_bound - low_bound)
    inverse_diag = level_info[4]
    if from_zero:
        residual_now = target
        update = inverse_diag * residual_now / center
        solution = update
    else:
        residual_now = target - apply_operator(start, level_info, assembler)
        update = inverse_diag * residual_now / center
        solution = start + update
    residual_now = residual_now - apply_operator(update, level_info, assembler)
    rho_first = half_width / center
    rho_next = 1.0 / (2.0 * center / half_width - rho_first)
    update = (
        rho_next * rho_first * update + 2.0 * rho_next / half_width * inverse_diag * residual_now
    )
    return solution + update


def restrict(values, coarse_count, fine_count):
    matrix = interpolation(coarse_count, fine_count).T
    return along_third(along_second(along_first(values, matrix), matrix), matrix)


def prolong(values, coarse_count, fine_count):
    matrix = interpolation(coarse_count, fine_count)
    return along_third(along_second(along_first(values, matrix), matrix), matrix)


def conjugate_gradients(target, level_info, assembler, reduce_sum):
    node_weight = level_info[3]
    norm_start = reduce_sum(jnp.sum(node_weight * target * target))

    def iterate(index, cg_state):
        solution, residual_now, direction, norm_now = cg_state
        applied = apply_operator(direction, level_info, assembler)
        step_len = norm_now / reduce_sum(jnp.sum(node_weight * direction * applied))
        solution = solution + step_len * direction
        residual_now = residual_now - step_len * applied
        norm_next = reduce_sum(jnp.sum(node_weight * residual_now * residual_now))
        direction = residual_now + norm_next / norm_now * direction
        return (solution, residual_now, direction, norm_next)

    final_state = lax.fori_loop(
        0, CG_ITERS, iterate, (jnp.zeros_like(target), target, target, norm_start)
    )
    return final_state[0]


def sum_spread(partial_sum):
    return lax.psum(partial_sum, ("gx", "gy"))


def coarse_spread(target, level_info):
    return conjugate_gradients(target, level_info, assemble, sum_spread)


def per_device(pressure_source, building_heights):
    side_first = pressure_source.shape[0] // 6
    side_second = pressure_source.shape[1] // 6
    column = pressure_source.shape[2] // 6
    start_first = lax.axis_index("gx") * side_first
    start_second = lax.axis_index("gy") * side_second
    heights_pad = jnp.pad(building_heights, 1, constant_values=column)
    local_heights = lax.dynamic_slice(
        heights_pad, (start_first, start_second), (side_first + 2, side_second + 2)
    )
    exist_cols = lax.dynamic_slice(
        jnp.pad(jnp.ones(building_heights.shape, jnp.float32), 1),
        (start_first, start_second),
        (side_first + 2, side_second + 2),
    )
    layers = jnp.arange(-1, column + 1, dtype=jnp.int32)
    inside = ((layers >= 0) & (layers < column)).astype(jnp.float32)[None, None, :]
    fluid_pad = (layers[None, None, :] >= local_heights[:, :, None]).astype(jnp.float32) * inside
    exist_pad = exist_cols[:, :, None] * inside
    fine_level = level_data(fluid_pad, exist_pad, 6)
    middle_level = level_data(fluid_pad, exist_pad, 4)
    coarse_level = level_data(fluid_pad, exist_pad, 2)
    fine_bounds = chebyshev_bounds(6)
    middle_bounds = chebyshev_bounds(4)
    target_fine = fine_level[2] * assemble(pressure_source, 6)
    fine_sol = smooth(target_fine, None, fine_level, fine_bounds, assemble, True)
    fine_res = target_fine - apply_operator(fine_sol, fine_level, assemble)
    target_middle = middle_level[2] * assemble(restrict(fine_level[3] * fine_res, 4, 6), 4)
    middle_sol = smooth(target_middle, None, middle_level, middle_bounds, assemble, True)
    middle_res = target_middle - apply_operator(middle_sol, middle_level, assemble)
    target_coarse = coarse_level[2] * assemble(restrict(middle_level[3] * middle_res, 2, 4), 2)
    coarse_sol = coarse_spread(target_coarse, coarse_level)
    middle_sol = middle_sol + middle_level[2] * prolong(coarse_sol, 2, 4)
    middle_sol = smooth(target_middle, middle_sol, middle_level, middle_bounds, assemble, False)
    fine_sol = fine_sol + fine_level[2] * prolong(middle_sol, 4, 6)
    fine_sol = smooth(target_fine, fine_sol, fine_level, fine_bounds, assemble, False)
    return (fine_sol, coarse_sol)


def solution(mesh):
    in_specs = (P("gx", "gy", None), P())
    out_specs = (P("gx", "gy", None), P("gx", "gy", None))
    return jax.shard_map(
        per_device, mesh=mesh, in_specs=in_specs, out_specs=out_specs, check_vma=False
    )
```

profile of v0, /device:TPU:105, one launch (start us, length us, event | category | flops | bytes accessed | tf_op | source)
XLA Modules:
  0.0 2164.7 jit_solution(11092381032411942674)
XLA Ops:
  275.1 5.7 collective-permute-start.26
  328.0 63.3 %psum.27 = f32[]{:T(128)} all-reduce(f32[]{:T(128)} %get-tuple-element.560), channel_id=1, replica_groups=mesh['gx'=8,'gy'=16] {'gx','gy'}, use_global_device_ids=true, to_apply=%region_1.2 | all-reduce | flops 1 | bytes 8 | tf_op jit(solution)/shard_map/psum | solution.py:300
  391.3 1636.0 %while.23 = (s32[]{:T(128)}, f32[8,8,128]{2,1,0:T(8,128)}, f32[8,8,128]{2,1,0:T(8,128)}, f32[8,8,128]{2,1,0:T(8,128)S(1)}, f32[]{:T(128)}, /*index=5*/f32[8,8,64...) while((s32[]{:T(128)}, f32[8,8,128]{2,1,0:T(8,128)}, ...), condition=%wide.region_7.8_spmd.clone.clone.clone.clone.clone, body=%wide.region_2.7_spmd.sunk.clone.clone.clone.clone.clone.sunk | while | flops 13401093 | bytes 2653795 | solution.py:293
  405.7 5.5 collective-permute-start.3
  424.1 63.5 %psum.42 = f32[]{:T(128)} all-reduce(f32[]{:T(128)} %get-tuple-element.823), channel_id=1, replica_groups=mesh['gx'=8,'gy'=16] {'gx','gy'}, use_global_device_ids=true, to_apply=%region_4.4 | all-reduce | flops 1 | bytes 8 | tf_op jit(solution)/shard_map/while/body/eval_jaxpr/psum | solution.py:300
  490.4 62.5 %psum.43 = f32[]{:T(128)} all-reduce(f32[]{:T(128)} %get-tuple-element.825), channel_id=1, replica_groups=mesh['gx'=8,'gy'=16] {'gx','gy'}, use_global_device_ids=true, to_apply=%region_6.6 | all-reduce | flops 1 | bytes 8 | tf_op jit(solution)/shard_map/while/body/eval_jaxpr/psum | solution.py:300
  587.4 63.8 %psum.42 = f32[]{:T(128)} all-reduce(f32[]{:T(128)} %get-tuple-element.823), channel_id=1, replica_groups=mesh['gx'=8,'gy'=16] {'gx','gy'}, use_global_device_ids=true, to_apply=%region_4.4 | all-reduce | flops 1 | bytes 8 | tf_op jit(solution)/shard_map/while/body/eval_jaxpr/psum | solution.py:300
  653.9 62.5 %psum.43 = f32[]{:T(128)} all-reduce(f32[]{:T(128)} %get-tuple-element.825), channel_id=1, replica_groups=mesh['gx'=8,'gy'=16] {'gx','gy'}, use_global_device_ids=true, to_apply=%region_6.6 | all-reduce | flops 1 | bytes 8 | tf_op jit(solution)/shard_map/while/body/eval_jaxpr/psum | solution.py:300
  751.2 63.5 %psum.42 = f32[]{:T(128)} all-reduce(f32[]{:T(128)} %get-tuple-element.823), channel_id=1, replica_groups=mesh['gx'=8,'gy'=16] {'gx','gy'}, use_global_device_ids=true, to_apply=%region_4.4 | all-reduce | flops 1 | bytes 8 | tf_op jit(solution)/shard_map/while/body/eval_jaxpr/psum | solution.py:300
  817.5 62.5 %psum.43 = f32[]{:T(128)} all-reduce(f32[]{:T(128)} %get-tuple-element.825), channel_id=1, replica_groups=mesh['gx'=8,'gy'=16] {'gx','gy'}, use_global_device_ids=true, to_apply=%region_6.6 | all-reduce | flops 1 | bytes 8 | tf_op jit(solution)/shard_map/while/body/eval_jaxpr/psum | solution.py:300
  914.8 63.6 %psum.42 = f32[]{:T(128)} all-reduce(f32[]{:T(128)} %get-tuple-element.823), channel_id=1, replica_groups=mesh['gx'=8,'gy'=16] {'gx','gy'}, use_global_device_ids=true, to_apply=%region_4.4 | all-reduce | flops 1 | bytes 8 | tf_op jit(solution)/shard_map/while/body/eval_jaxpr/psum | solution.py:300
  981.1 62.5 %psum.43 = f32[]{:T(128)} all-reduce(f32[]{:T(128)} %get-tuple-element.825), channel_id=1, replica_groups=mesh['gx'=8,'gy'=16] {'gx','gy'}, use_global_device_ids=true, to_apply=%region_6.6 | all-reduce | flops 1 | bytes 8 | tf_op jit(solution)/shard_map/while/body/eval_jaxpr/psum | solution.py:300
  1078.4 63.6 %psum.42 = f32[]{:T(128)} all-reduce(f32[]{:T(128)} %get-tuple-element.823), channel_id=1, replica_groups=mesh['gx'=8,'gy'=16] {'gx','gy'}, use_global_device_ids=true, to_apply=%region_4.4 | all-reduce | flops 1 | bytes 8 | tf_op jit(solution)/shard_map/while/body/eval_jaxpr/psum | solution.py:300
  1144.7 62.5 %psum.43 = f32[]{:T(128)} all-reduce(f32[]{:T(128)} %get-tuple-element.825), channel_id=1, replica_groups=mesh['gx'=8,'gy'=16] {'gx','gy'}, use_global_device_ids=true, to_apply=%region_6.6 | all-reduce | flops 1 | bytes 8 | tf_op jit(solution)/shard_map/while/body/eval_jaxpr/psum | solution.py:300
  1242.0 63.6 %psum.42 = f32[]{:T(128)} all-reduce(f32[]{:T(128)} %get-tuple-element.823), channel_id=1, replica_groups=mesh['gx'=8,'gy'=16] {'gx','gy'}, use_global_device_ids=true, to_apply=%region_4.4 | all-reduce | flops 1 | bytes 8 | tf_op jit(solution)/shard_map/while/body/eval_jaxpr/psum | solution.py:300
  1308.3 62.5 %psum.43 = f32[]{:T(128)} all-reduce(f32[]{:T(128)} %get-tuple-element.825), channel_id=1, replica_groups=mesh['gx'=8,'gy'=16] {'gx','gy'}, use_global_device_ids=true, to_apply=%region_6.6 | all-reduce | flops 1 | bytes 8 | tf_op jit(solution)/shard_map/while/body/eval_jaxpr/psum | solution.py:300
  1405.6 63.6 %psum.42 = f32[]{:T(128)} all-reduce(f32[]{:T(128)} %get-tuple-element.823), channel_id=1, replica_groups=mesh['gx'=8,'gy'=16] {'gx','gy'}, use_global_device_ids=true, to_apply=%region_4.4 | all-reduce | flops 1 | bytes 8 | tf_op jit(solution)/shard_map/while/body/eval_jaxpr/psum | solution.py:300
  1471.8 62.5 %psum.43 = f32[]{:T(128)} all-reduce(f32[]{:T(128)} %get-tuple-element.825), channel_id=1, replica_groups=mesh['gx'=8,'gy'=16] {'gx','gy'}, use_global_device_ids=true, to_apply=%region_6.6 | all-reduce | flops 1 | bytes 8 | tf_op jit(solution)/shard_map/while/body/eval_jaxpr/psum | solution.py:300
  1569.2 63.6 %psum.42 = f32[]{:T(128)} all-reduce(f32[]{:T(128)} %get-tuple-element.823), channel_id=1, replica_groups=mesh['gx'=8,'gy'=16] {'gx','gy'}, use_global_device_ids=true, to_apply=%region_4.4 | all-reduce | flops 1 | bytes 8 | tf_op jit(solution)/shard_map/while/body/eval_jaxpr/psum | solution.py:300
  1635.4 62.5 %psum.43 = f32[]{:T(128)} all-reduce(f32[]{:T(128)} %get-tuple-element.825), channel_id=1, replica_groups=mesh['gx'=8,'gy'=16] {'gx','gy'}, use_global_device_ids=true, to_apply=%region_6.6 | all-reduce | flops 1 | bytes 8 | tf_op jit(solution)/shard_map/while/body/eval_jaxpr/psum | solution.py:300
  1732.7 63.6 %psum.42 = f32[]{:T(128)} all-reduce(f32[]{:T(128)} %get-tuple-element.823), channel_id=1, replica_groups=mesh['gx'=8,'gy'=16] {'gx','gy'}, use_global_device_ids=true, to_apply=%region_4.4 | all-reduce | flops 1 | bytes 8 | tf_op jit(solution)/shard_map/while/body/eval_jaxpr/psum | solution.py:300
  1799.0 62.5 %psum.43 = f32[]{:T(128)} all-reduce(f32[]{:T(128)} %get-tuple-element.825), channel_id=1, replica_groups=mesh['gx'=8,'gy'=16] {'gx','gy'}, use_global_device_ids=true, to_apply=%region_6.6 | all-reduce | flops 1 | bytes 8 | tf_op jit(solution)/shard_map/while/body/eval_jaxpr/psum | solution.py:300
  1896.3 63.6 %psum.42 = f32[]{:T(128)} all-reduce(f32[]{:T(128)} %get-tuple-element.823), channel_id=1, replica_groups=mesh['gx'=8,'gy'=16] {'gx','gy'}, use_global_device_ids=true, to_apply=%region_4.4 | all-reduce | flops 1 | bytes 8 | tf_op jit(solution)/shard_map/while/body/eval_jaxpr/psum | solution.py:300
  1962.6 62.5 %psum.43 = f32[]{:T(128)} all-reduce(f32[]{:T(128)} %get-tuple-element.825), channel_id=1, replica_groups=mesh['gx'=8,'gy'=16] {'gx','gy'}, use_global_device_ids=true, to_apply=%region_6.6 | all-reduce | flops 1 | bytes 8 | tf_op jit(solution)/shard_map/while/body/eval_jaxpr/psum | solution.py:300
  (1167 shorter events, 802.1 us)
Async XLA Ops:
  13.1 59.8 %collective-permute-start.6 = (f32[26,1,384]{2,1,0:T(1,128)}, f32[26,1,384]{2,1,0:T(1,128)}, u32[]{:S(2)}, u32[]{:S(2)}) collective-permute-start(f32[26,1,384]{2,1,0:T(1,128)} %get-tuple-element.590), channel_id=1, source_target_pairs={{0,1},{1,2},{2,3},{3,4},{4,5},{5,6},{6,7},{7,8},{8,9},{9,10},{10,1... | collective-permute-start | bytes 119816 | tf_op jit(solution)/shard_map/ppermute | solution.py:19
  15.0 57.9 %collective-permute-start.7 = (f32[26,1,384]{2,1,0:T(1,128)}, f32[26,1,384]{2,1,0:T(1,128)}, u32[]{:S(2)}, u32[]{:S(2)}) collective-permute-start(f32[26,1,384]{2,1,0:T(1,128)} %get-tuple-element.591), channel_id=1, source_target_pairs={{1,0},{2,1},{3,2},{4,3},{5,4},{6,5},{7,6},{8,7},{9,8},{10,9},{11,1... | collective-permute-start | bytes 119816 | tf_op jit(solution)/shard_map/ppermute | solution.py:21
  168.8 49.5 %collective-permute-start.18 = (f32[18,1,256]{2,1,0:T(1,128)}, f32[18,1,256]{2,1,0:T(1,128)}, u32[]{:S(2)}, u32[]{:S(2)}) collective-permute-start(f32[18,1,256]{2,1,0:T(1,128)} %get-tuple-element.620), channel_id=1, source_target_pairs={{0,1},{1,2},{2,3},{3,4},{4,5},{5,6},{6,7},{7,8},{8,9},{9,10},{10,1... | collective-permute-start | bytes 55304 | tf_op jit(solution)/shard_map/ppermute | solution.py:19
  170.7 47.6 %collective-permute-start.19 = (f32[18,1,256]{2,1,0:T(1,128)}, f32[18,1,256]{2,1,0:T(1,128)}, u32[]{:S(2)}, u32[]{:S(2)}) collective-permute-start(f32[18,1,256]{2,1,0:T(1,128)} %get-tuple-element.621), channel_id=1, source_target_pairs={{1,0},{2,1},{3,2},{4,3},{5,4},{6,5},{7,6},{8,7},{9,8},{10,9},{11,1... | collective-permute-start | bytes 55304 | tf_op jit(solution)/shard_map/ppermute | solution.py:21
  299.8 23.9 %collective-permute-start.30 = (f32[10,1,128]{2,1,0:T(1,128)}, f32[10,1,128]{2,1,0:T(1,128)}, u32[]{:S(2)}, u32[]{:S(2)}) collective-permute-start(f32[10,1,128]{2,1,0:T(1,128)} %get-tuple-element.666), channel_id=1, source_target_pairs={{0,1},{1,2},{2,3},{3,4},{4,5},{5,6},{6,7},{7,8},{8,9},{9,10},{10,1... | collective-permute-start | bytes 15368 | tf_op jit(solution)/shard_map/ppermute | solution.py:19
  301.7 22.0 %collective-permute-start.31 = (f32[10,1,128]{2,1,0:T(1,128)}, f32[10,1,128]{2,1,0:T(1,128)}, u32[]{:S(2)}, u32[]{:S(2)}) collective-permute-start(f32[10,1,128]{2,1,0:T(1,128)} %get-tuple-element.667), channel_id=1, source_target_pairs={{1,0},{2,1},{3,2},{4,3},{5,4},{6,5},{7,6},{8,7},{9,8},{10,9},{11,1... | collective-permute-start | bytes 15368 | tf_op jit(solution)/shard_map/ppermute | solution.py:21
  403.8 18.0 collective-permute-start.2
  405.7 16.1 collective-permute-start.3
  567.1 18.0 collective-permute-start.2
  730.9 18.0 collective-permute-start.2
  733.6 15.3 collective-permute-start.3
  894.4 18.0 collective-permute-start.2
  897.2 15.3 collective-permute-start.3
  1058.0 18.0 collective-permute-start.2
  1060.8 15.3 collective-permute-start.3
  1221.6 18.0 collective-permute-start.2
  1224.3 15.3 collective-permute-start.3
  1385.2 18.0 collective-permute-start.2
  1548.8 18.0 collective-permute-start.2
  1551.5 15.3 collective-permute-start.3
  1712.4 18.0 collective-permute-start.2
  1715.1 15.3 collective-permute-start.3
  1876.0 18.0 collective-permute-start.2
  1878.7 15.3 collective-permute-start.3
  (265 other events, 1763.4 us)
where the time goes:
time: 2180 us; the launch traced here: 2160 us
  blocking collectives  1320 us (61%)
  local copies, waits for them, and re-layouts  303 us (14%)
  starting transfers between devices  256 us (12%)
  other arithmetic  103 us (5%)
  matrix products  92.5 us (4%)
  waiting for transfers between devices  59.1 us (3%)
  loops' own time  22.8 us (1%)
    psum x21, blocking collectives, sum_spread(): return lax.psum(partial_sum, ('gx', 'gy'))  1320 us
    ppermute x42, starting transfers between devices, with_halo(): lax.ppermute(tail, axis, [(i, (i + 1) % count) for i in range(ends)])  150 us
    ppermute x42, starting transfers between devices, with_halo(): lax.ppermute(head, axis, [((i + 1) % count, i) for i in range(ends)])  106 us
    mul x58, local copies, waits for them, and re-layouts, spread_counts(): at_end * step_two[:, :, 2:][:, :, :, None]  67 us
    add x52, local copies, waits for them, and re-layouts, spread_counts(): step_two[:, :, 1:-1][:, :, :, None]  64.9 us
    mul x58, local copies, waits for them, and re-layouts, spread_counts(): at_start * step_two[:, :, :-2][:, :, :, None]  54.8 us
    ppermute x42, waiting for transfers between devices, with_halo(): lax.ppermute(head, axis, [((i + 1) % count, i) for i in range(ends)])  51.8 us
  transfers between devices with their start and end apart: 84, of which 26 were waited for; matrix products, arithmetic and copies ran while one was open for 11% of the time, Pallas kernels for 0%

commit v1 on v0

--- a/solution.py
+++ b/solution.py
@@ -6,6 +6,11 @@
 
 CG_ITERS = 10
 HIGHEST = lax.Precision.HIGHEST
+
+
+def one_after_other(x, axis_one, axis_two):
+    partial = lax.psum(x, axis_one)
+    return lax.psum(partial, axis_two)
 
 
 def with_halo(cells, sides, width):
@@ -297,7 +302,7 @@
 
 
 def sum_spread(partial_sum):
-    return lax.psum(partial_sum, ("gx", "gy"))
+    return one_after_other(partial_sum, "gy", "gx")
 
 
 def coarse_spread(target, level_info):

time: 2180 us -> 1870 us (0.86)
  blocking collectives: 1320 us -> 1010 us
    psum x21 -> x42, blocking collectives: 1320 us -> 1010 us  [the longest x21 599 us: one_after_other(): partial = lax.psum(x, axis_one)]
    ppermute x42, starting transfers between devices: 150 us -> 126 us  [with_halo(): lax.ppermute(tail, axis, [(i, (i + 1) % count) for i in range(ends)])]
  transfers between devices with their start and end apart: 84 -> 84, of which waited for: 26 -> 28; matrix products, arithmetic and copies ran while one was open for 11% -> 12% of each run, Pallas kernels for 0% -> 0%
where the time goes in v1:
time: 1870 us; the launch traced here: 1850 us
  blocking collectives  1010 us (54%)
  local copies, waits for them, and re-layouts  306 us (16%)
  starting transfers between devices  248 us (13%)
  other arithmetic  101 us (5%)
  matrix products  92.5 us (5%)
  waiting for transfers between devices  63.6 us (3%)
  loops' own time  22.2 us (1%)
    psum x21, blocking collectives, one_after_other(): partial = lax.psum(x, axis_one)  599 us
    psum x21, blocking collectives, one_after_other(): return lax.psum(partial, axis_two)  415 us
    ppermute x42, starting transfers between devices, with_halo(): lax.ppermute(tail, axis, [(i, (i + 1) % count) for i in range(ends)])  126 us
    ppermute x42, starting transfers between devices, with_halo(): lax.ppermute(head, axis, [((i + 1) % count, i) for i in range(ends)])  122 us
    mul x58, local copies, waits for them, and re-layouts, spread_counts(): at_end * step_two[:, :, 2:][:, :, :, None]  69.8 us
    add x52, local copies, waits for them, and re-layouts, spread_counts(): step_two[:, :, 1:-1][:, :, :, None]  66.9 us
    mul x58, local copies, waits for them, and re-layouts, spread_counts(): at_start * step_two[:, :, :-2][:, :, :, None]  57.4 us
    ppermute x42, waiting for transfers between devices, with_halo(): lax.ppermute(head, axis, [((i + 1) % count, i) for i in range(ends)])  56.3 us
  transfers between devices with their start and end apart: 84, of which 28 were waited for; matrix products, arithmetic and copies ran while one was open for 12% of the time, Pallas kernels for 0%

profile of v1, /device:TPU:105, one launch (start us, length us, event | category | flops | bytes accessed | tf_op | source)
XLA Modules:
  0.0 1851.7 jit_solution(17920811781715666761)
XLA Ops:
  329.8 24.4 %psum.54 = f32[]{:T(128)} all-reduce(f32[]{:T(128)} %get-tuple-element.560), channel_id=1, replica_groups=mesh['gx'=8,'gy'=16] {'gy'}, use_global_device_ids=true, to_apply=%region_1.2 | all-reduce | flops 1 | bytes 8 | tf_op jit(solution)/shard_map/psum | solution.py:12
  373.6 1340.5 %while.23 = (s32[]{:T(128)}, f32[8,8,128]{2,1,0:T(8,128)}, f32[8,8,128]{2,1,0:T(8,128)}, f32[8,8,128]{2,1,0:T(8,128)S(1)}, f32[]{:T(128)}, /*index=5*/f32[8,8,64...) while((s32[]{:T(128)}, f32[8,8,128]{2,1,0:T(8,128)}, ...), condition=%wide.region_10.11_spmd.clone.clone.clone.clone.clone, body=%wide.region_3.10_spmd.sunk.clone.clone.clone.clone.clone.sunk | while | flops 13401095 | bytes 2653811 | solution.py:298
  406.0 24.4 %psum.84 = f32[]{:T(128)} all-reduce(f32[]{:T(128)} %get-tuple-element.823), channel_id=1, replica_groups=mesh['gx'=8,'gy'=16] {'gy'}, use_global_device_ids=true, to_apply=%region_5.5 | all-reduce | flops 1 | bytes 8 | tf_op jit(solution)/shard_map/while/body/eval_jaxpr/psum | solution.py:12
  452.4 28.1 %psum.86 = f32[]{:T(128)} all-reduce(f32[]{:T(128)} %get-tuple-element.825), channel_id=1, replica_groups=mesh['gx'=8,'gy'=16] {'gy'}, use_global_device_ids=true, to_apply=%region_8.8 | all-reduce | flops 1 | bytes 8 | tf_op jit(solution)/shard_map/while/body/eval_jaxpr/psum | solution.py:12
  534.3 28.8 %psum.84 = f32[]{:T(128)} all-reduce(f32[]{:T(128)} %get-tuple-element.823), channel_id=1, replica_groups=mesh['gx'=8,'gy'=16] {'gy'}, use_global_device_ids=true, to_apply=%region_5.5 | all-reduce | flops 1 | bytes 8 | tf_op jit(solution)/shard_map/while/body/eval_jaxpr/psum | solution.py:12
  585.4 29.2 %psum.86 = f32[]{:T(128)} all-reduce(f32[]{:T(128)} %get-tuple-element.825), channel_id=1, replica_groups=mesh['gx'=8,'gy'=16] {'gy'}, use_global_device_ids=true, to_apply=%region_8.8 | all-reduce | flops 1 | bytes 8 | tf_op jit(solution)/shard_map/while/body/eval_jaxpr/psum | solution.py:12
  614.6 20.0 %psum.87 = f32[]{:T(128)} all-reduce(f32[]{:T(128)} %psum.86), channel_id=1, replica_groups=mesh['gx'=8,'gy'=16] {'gx'}, use_global_device_ids=true, to_apply=%region_9.9 | all-reduce | flops 1 | bytes 8 | tf_op jit(solution)/shard_map/while/body/eval_jaxpr/psum | solution.py:13
  668.9 28.8 %psum.84 = f32[]{:T(128)} all-reduce(f32[]{:T(128)} %get-tuple-element.823), channel_id=1, replica_groups=mesh['gx'=8,'gy'=16] {'gy'}, use_global_device_ids=true, to_apply=%region_5.5 | all-reduce | flops 1 | bytes 8 | tf_op jit(solution)/shard_map/while/body/eval_jaxpr/psum | solution.py:12
  720.1 29.2 %psum.86 = f32[]{:T(128)} all-reduce(f32[]{:T(128)} %get-tuple-element.825), channel_id=1, replica_groups=mesh['gx'=8,'gy'=16] {'gy'}, use_global_device_ids=true, to_apply=%region_8.8 | all-reduce | flops 1 | bytes 8 | tf_op jit(solution)/shard_map/while/body/eval_jaxpr/psum | solution.py:12
  749.3 20.0 %psum.87 = f32[]{:T(128)} all-reduce(f32[]{:T(128)} %psum.86), channel_id=1, replica_groups=mesh['gx'=8,'gy'=16] {'gx'}, use_global_device_ids=true, to_apply=%region_9.9 | all-reduce | flops 1 | bytes 8 | tf_op jit(solution)/shard_map/while/body/eval_jaxpr/psum | solution.py:13
  803.6 28.8 %psum.84 = f32[]{:T(128)} all-reduce(f32[]{:T(128)} %get-tuple-element.823), channel_id=1, replica_groups=mesh['gx'=8,'gy'=16] {'gy'}, use_global_device_ids=true, to_apply=%region_5.5 | all-reduce | flops 1 | bytes 8 | tf_op jit(solution)/shard_map/while/body/eval_jaxpr/psum | solution.py:12
  854.7 29.2 %psum.86 = f32[]{:T(128)} all-reduce(f32[]{:T(128)} %get-tuple-element.825), channel_id=1, replica_groups=mesh['gx'=8,'gy'=16] {'gy'}, use_global_device_ids=true, to_apply=%region_8.8 | all-reduce | flops 1 | bytes 8 | tf_op jit(solution)/shard_map/while/body/eval_jaxpr/psum | solution.py:12
  938.2 28.8 %psum.84 = f32[]{:T(128)} all-reduce(f32[]{:T(128)} %get-tuple-element.823), channel_id=1, replica_groups=mesh['gx'=8,'gy'=16] {'gy'}, use_global_device_ids=true, to_apply=%region_5.5 | all-reduce | flops 1 | bytes 8 | tf_op jit(solution)/shard_map/while/body/eval_jaxpr/psum | solution.py:12
  989.4 29.2 %psum.86 = f32[]{:T(128)} all-reduce(f32[]{:T(128)} %get-tuple-element.825), channel_id=1, replica_groups=mesh['gx'=8,'gy'=16] {'gy'}, use_global_device_ids=true, to_apply=%region_8.8 | all-reduce | flops 1 | bytes 8 | tf_op jit(solution)/shard_map/while/body/eval_jaxpr/psum | solution.py:12
  1072.9 28.8 %psum.84 = f32[]{:T(128)} all-reduce(f32[]{:T(128)} %get-tuple-element.823), channel_id=1, replica_groups=mesh['gx'=8,'gy'=16] {'gy'}, use_global_device_ids=true, to_apply=%region_5.5 | all-reduce | flops 1 | bytes 8 | tf_op jit(solution)/shard_map/while/body/eval_jaxpr/psum | solution.py:12
  1124.1 29.2 %psum.86 = f32[]{:T(128)} all-reduce(f32[]{:T(128)} %get-tuple-element.825), channel_id=1, replica_groups=mesh['gx'=8,'gy'=16] {'gy'}, use_global_device_ids=true, to_apply=%region_8.8 | all-reduce | flops 1 | bytes 8 | tf_op jit(solution)/shard_map/while/body/eval_jaxpr/psum | solution.py:12
  1207.6 28.8 %psum.84 = f32[]{:T(128)} all-reduce(f32[]{:T(128)} %get-tuple-element.823), channel_id=1, replica_groups=mesh['gx'=8,'gy'=16] {'gy'}, use_global_device_ids=true, to_apply=%region_5.5 | all-reduce | flops 1 | bytes 8 | tf_op jit(solution)/shard_map/while/body/eval_jaxpr/psum | solution.py:12
  1258.7 29.2 %psum.86 = f32[]{:T(128)} all-reduce(f32[]{:T(128)} %get-tuple-element.825), channel_id=1, replica_groups=mesh['gx'=8,'gy'=16] {'gy'}, use_global_device_ids=true, to_apply=%region_8.8 | all-reduce | flops 1 | bytes 8 | tf_op jit(solution)/shard_map/while/body/eval_jaxpr/psum | solution.py:12
  1342.2 28.8 %psum.84 = f32[]{:T(128)} all-reduce(f32[]{:T(128)} %get-tuple-element.823), channel_id=1, replica_groups=mesh['gx'=8,'gy'=16] {'gy'}, use_global_device_ids=true, to_apply=%region_5.5 | all-reduce | flops 1 | bytes 8 | tf_op jit(solution)/shard_map/while/body/eval_jaxpr/psum | solution.py:12
  1393.4 29.2 %psum.86 = f32[]{:T(128)} all-reduce(f32[]{:T(128)} %get-tuple-element.825), channel_id=1, replica_groups=mesh['gx'=8,'gy'=16] {'gy'}, use_global_device_ids=true, to_apply=%region_8.8 | all-reduce | flops 1 | bytes 8 | tf_op jit(solution)/shard_map/while/body/eval_jaxpr/psum | solution.py:12
  1476.9 28.8 %psum.84 = f32[]{:T(128)} all-reduce(f32[]{:T(128)} %get-tuple-element.823), channel_id=1, replica_groups=mesh['gx'=8,'gy'=16] {'gy'}, use_global_device_ids=true, to_apply=%region_5.5 | all-reduce | flops 1 | bytes 8 | tf_op jit(solution)/shard_map/while/body/eval_jaxpr/psum | solution.py:12
  1528.0 29.2 %psum.86 = f32[]{:T(128)} all-reduce(f32[]{:T(128)} %get-tuple-element.825), channel_id=1, replica_groups=mesh['gx'=8,'gy'=16] {'gy'}, use_global_device_ids=true, to_apply=%region_8.8 | all-reduce | flops 1 | bytes 8 | tf_op jit(solution)/shard_map/while/body/eval_jaxpr/psum | solution.py:12
  1611.6 28.8 %psum.84 = f32[]{:T(128)} all-reduce(f32[]{:T(128)} %get-tuple-element.823), channel_id=1, replica_groups=mesh['gx'=8,'gy'=16] {'gy'}, use_global_device_ids=true, to_apply=%region_5.5 | all-reduce | flops 1 | bytes 8 | tf_op jit(solution)/shard_map/while/body/eval_jaxpr/psum | solution.py:12
  1662.7 29.2 %psum.86 = f32[]{:T(128)} all-reduce(f32[]{:T(128)} %get-tuple-element.825), channel_id=1, replica_groups=mesh['gx'=8,'gy'=16] {'gy'}, use_global_device_ids=true, to_apply=%region_8.8 | all-reduce | flops 1 | bytes 8 | tf_op jit(solution)/shard_map/while/body/eval_jaxpr/psum | solution.py:12
  (1238 shorter events, 1185.9 us)
Async XLA Ops:
  13.1 59.8 %collective-permute-start.6 = (f32[26,1,384]{2,1,0:T(1,128)}, f32[26,1,384]{2,1,0:T(1,128)}, u32[]{:S(2)}, u32[]{:S(2)}) collective-permute-start(f32[26,1,384]{2,1,0:T(1,128)} %get-tuple-element.590), channel_id=1, source_target_pairs={{0,1},{1,2},{2,3},{3,4},{4,5},{5,6},{6,7},{7,8},{8,9},{9,10},{10,1... | collective-permute-start | bytes 119816 | tf_op jit(solution)/shard_map/ppermute | solution.py:24
  15.0 57.9 %collective-permute-start.7 = (f32[26,1,384]{2,1,0:T(1,128)}, f32[26,1,384]{2,1,0:T(1,128)}, u32[]{:S(2)}, u32[]{:S(2)}) collective-permute-start(f32[26,1,384]{2,1,0:T(1,128)} %get-tuple-element.591), channel_id=1, source_target_pairs={{1,0},{2,1},{3,2},{4,3},{5,4},{6,5},{7,6},{8,7},{9,8},{10,9},{11,1... | collective-permute-start | bytes 119816 | tf_op jit(solution)/shard_map/ppermute | solution.py:26
  170.2 55.3 %collective-permute-start.18 = (f32[18,1,256]{2,1,0:T(1,128)S(1)}, f32[18,1,256]{2,1,0:T(1,128)S(1)}, u32[]{:S(2)}, u32[]{:S(2)}) collective-permute-start(f32[18,1,256]{2,1,0:T(1,128)S(1)} %get-tuple-element.620), channel_id=1, source_target_pairs={{0,1},{1,2},{2,3},{3,4},{4,5},{5,6},{6,7},{7,8},{8,9},{9,10},{10,1... | collective-permute-start | bytes 55304 | tf_op jit(solution)/shard_map/ppermute | solution.py:24
  172.2 54.0 %collective-permute-start.19 = (f32[18,1,256]{2,1,0:T(1,128)S(1)}, f32[18,1,256]{2,1,0:T(1,128)}, u32[]{:S(2)}, u32[]{:S(2)}) collective-permute-start(f32[18,1,256]{2,1,0:T(1,128)S(1)} %get-tuple-element.621), channel_id=1, source_target_pairs={{1,0},{2,1},{3,2},{4,3},{5,4},{6,5},{7,6},{8,7},{9,8},{10,9},{11,1... | collective-permute-start | bytes 55304 | tf_op jit(solution)/shard_map/ppermute | solution.py:26
  301.7 24.5 %collective-permute-start.30 = (f32[10,1,128]{2,1,0:T(1,128)}, f32[10,1,128]{2,1,0:T(1,128)}, u32[]{:S(2)}, u32[]{:S(2)}) collective-permute-start(f32[10,1,128]{2,1,0:T(1,128)} %get-tuple-element.666), channel_id=1, source_target_pairs={{0,1},{1,2},{2,3},{3,4},{4,5},{5,6},{6,7},{7,8},{8,9},{9,10},{10,1... | collective-permute-start | bytes 15368 | tf_op jit(solution)/shard_map/ppermute | solution.py:24
  303.6 22.6 %collective-permute-start.31 = (f32[10,1,128]{2,1,0:T(1,128)}, f32[10,1,128]{2,1,0:T(1,128)}, u32[]{:S(2)}, u32[]{:S(2)}) collective-permute-start(f32[10,1,128]{2,1,0:T(1,128)} %get-tuple-element.667), channel_id=1, source_target_pairs={{1,0},{2,1},{3,2},{4,3},{5,4},{6,5},{7,6},{8,7},{9,8},{10,9},{11,1... | collective-permute-start | bytes 15368 | tf_op jit(solution)/shard_map/ppermute | solution.py:26
  385.5 18.2 collective-permute-start.2
  387.5 16.2 collective-permute-start.3
  514.0 18.0 collective-permute-start.2
  648.6 18.0 collective-permute-start.2
  653.2 13.4 collective-permute-start.3
  783.3 18.0 collective-permute-start.2
  918.0 18.0 collective-permute-start.2
  922.5 13.4 collective-permute-start.3
  1052.6 18.0 collective-permute-start.2
  1057.1 13.4 collective-permute-start.3
  1187.3 18.0 collective-permute-start.2
  1191.8 13.5 collective-permute-start.3
  1322.0 18.0 collective-permute-start.2
  1326.5 13.5 collective-permute-start.3
  1456.6 18.0 collective-permute-start.2
  1461.1 13.5 collective-permute-start.3
  1591.3 18.0 collective-permute-start.2
  1595.8 13.5 collective-permute-start.3
  (290 other events, 1935.8 us)
